TPU v7x, 512 devices: a whole 4x8x8 slice. The times are simulated.
512 devices in a mesh: island: 16 (over y, core), fsdp: 32 (over z, x).
Axes of the slice: x: 4, y: 8, z: 8, core: 2. Of those that a mesh axis runs over, the one named last changes fastest.
Arguments:
- delta: bfloat16 [16, 2048, 4096], P('island', 'fsdp'), may hold values from -6 to 6
- error: float32 [16, 2048, 4096], P('island', 'fsdp'), may hold values from -6 to 6
- param: bfloat16 [2048, 4096], P('fsdp'), may hold values from -6 to 6
- velocity: bfloat16 [2048, 4096], P('fsdp'), may hold values from -4 to 4
- piece_ids: int32 [32, 32, 16], P('fsdp'), may hold values from 0 to 2047, as said below
- piece_counts: int32 [32, 32], P('fsdp'), may hold values from 8 to 16, as said below
Outputs:
- new_error: float32 [16, 2048, 4096], P('island', 'fsdp')
- new_param: bfloat16 [2048, 4096], P('fsdp')
- new_velocity: bfloat16 [2048, 4096], P('fsdp')
- compressed: float32 [32, 32, 16, 128], P('fsdp')
Inputs may be any that keep to these rules, and one draw needn't show every extreme that they name: `piece_ids`: within one shard's lists all entries are distinct, entries past the count included; those are ignored. `piece_counts`: one owner receives exactly 16 live entries from every shard.
All inputs are finite; a program needn't handle non-finite values.
Results may differ from a plain program's by a relative error of at most 0.001.
Values sent between devices are 32-bit elements; how exact they have to be, the bound alone decides.
A program may use at most 64 MiB of HBM per device.

v0:
```python
import jax
import jax.numpy as jnp
from jax import lax
from jax.sharding import PartitionSpec as P

decay_rate = 0.9
outer_rate = 0.7
nesterov = 0.9
eps_value = 1e-06


def cosine_table(side):
    freq = jnp.arange(side, dtype=jnp.int32)[:, None].astype(jnp.float32)
    place = jnp.arange(side, dtype=jnp.int32)[None, :].astype(jnp.float32)
    scale = jnp.where(freq == 0.0, jnp.sqrt(1.0 / side), jnp.sqrt(2.0 / side))
    return scale * jnp.cos(jnp.pi * (2.0 * place + 1.0) * freq / (2.0 * side))


def transform(field, table, column_table):
    rows, width = field.shape
    side = table.shape[0]
    right = jnp.dot(field.reshape(-1, 128), column_table, precision=lax.Precision.HIGHEST)
    right = right.reshape(rows // side, side, width // 128, 128)
    left = jnp.einsum("kn,rnqj->rqkj", table, right, precision=lax.Precision.HIGHEST)
    return left.reshape(-1, 128)


def inverse(pieces, table, column_table, rows, width):
    side = table.shape[0]
    blocks = pieces.reshape(rows // side, width // 128, side, 128)
    left = jnp.einsum("kn,rqkj->rnqj", table, blocks, precision=lax.Precision.HIGHEST)
    back = jnp.dot(left.reshape(-1, 128), column_table.T, precision=lax.Precision.HIGHEST)
    return back.reshape(rows, width)


def normalize(values):
    return values / jnp.sqrt(jnp.mean(values * values, axis=-1, keepdims=True) + eps_value)


def island_norm(pieces):
    total = lax.psum(pieces, "island")
    return normalize(total)


def shards(delta, error, param, velocity, piece_ids, piece_counts):
    rows, width = param.shape
    table = cosine_table(64)
    column_table = jnp.kron(jnp.eye(2, dtype=jnp.float32), table.T)
    momentum = decay_rate * error[0] + delta[0].astype(jnp.float32)
    coefficients = transform(momentum, table, column_table)
    piece_list = piece_ids[0]
    owners, slots = piece_list.shape
    slot_index = jnp.arange(slots, dtype=jnp.int32)[None, :]
    active = (slot_index < piece_counts[0][:, None]).astype(jnp.float32)
    chosen = coefficients[piece_list] * active[..., None]
    flat_ids = piece_list.reshape(-1)
    arrived = lax.all_to_all(chosen, "fsdp", split_axis=0, concat_axis=0, tiled=True)
    compressed = island_norm(arrived)
    returned = lax.all_to_all(compressed, "fsdp", split_axis=0, concat_axis=0, tiled=True)
    kept_mask = (
        jnp.zeros((coefficients.shape[0],), jnp.float32).at[flat_ids].set(active.reshape(-1))
    )
    new_error = momentum - inverse(
        coefficients * kept_mask[:, None], table, column_table, rows, width
    )
    scattered = (
        jnp.zeros(coefficients.shape, jnp.float32).at[flat_ids].add(returned.reshape(-1, 128))
    )
    update = inverse(scattered, table, column_table, rows, width)
    moved = nesterov * velocity.astype(jnp.float32) + update
    new_velocity = moved.astype(jnp.bfloat16)
    new_param = (param.astype(jnp.float32) - outer_rate * (update + nesterov * moved)).astype(
        jnp.bfloat16
    )
    return (new_error[None], new_param, new_velocity, compressed[None])


def solution(mesh):
    in_specs = (
        P("island", "fsdp", None),
        P("island", "fsdp", None),
        P("fsdp", None),
        P("fsdp", None),
        P("fsdp", None, None),
        P("fsdp", None),
    )
    out_specs = (
        P("island", "fsdp", None),
        P("fsdp", None),
        P("fsdp", None),
        P("fsdp", None, None, None),
    )
    return jax.shard_map(shards, mesh=mesh, in_specs=in_specs, out_specs=out_specs, check_vma=False)
```

profile of v0, /device:TPU:24, one launch (start us, length us, event | category | flops | bytes accessed | tf_op | source)
XLA Modules:
  0.0 192.9 jit_solution(322883646928115541)
XLA Ops:
  7.2 0.8 compare_select_fusion
  8.1 0.7 fusion.26
  9.4 1.3 fusion.6
  10.9 1.6 fusion.2
  12.6 1.2 fusion.12
  13.8 1.0 gather_fusion
  14.8 0.8 broadcast_multiply_fusion
  15.7 13.2 %all-to-all-start = ((f32[32,16,128]{2,1,0:T(8,128)}), f32[32,16,128]{2,1,0:T(8,128)S(1)}, u32[]{:S(2)}, u32[]{:S(2)}) async-start(f32[32,16,128]{2,1,0:T(8,128)} %broadcast_multiply_fusion), calls=%async_computation | async-start | bytes 524288 | tf_op jit(solution)/shard_map/all_to_all | solution.py:57
  29.8 2.5 %scatter_custom_fusion = f32[2048]{0:T(1024)S(1)} fusion(s32[512]{0:T(512)S(1)} %bitcast.60, f32[512]{0:T(512)S(1)} %reshape.275, f32[]{:T(128)} %constant.13.clone.1), kind=kCustom, calls=%fused_computation.46 | custom fusion | bytes 8196 | tf_op jit(solution)/shard_map/scatter | solution.py:61
  32.4 1.3 convolution_bitcast_fusion.1
  34.3 7.2 %all-to-all-done = f32[32,16,128]{2,1,0:T(8,128)S(1)} async-done(((f32[32,16,128]{2,1,0:T(8,128)}), f32[32,16,128]{2,1,0:T(8,128)S(1)}, u32[]{:S(2)}, u32[]{:S(2)}) %all-to-all-start) | async-done | bytes 262176 | tf_op jit(solution)/shard_map/all_to_all | solution.py:57
  42.3 1.0 fusion.32
  43.5 107.5 %all-reduce.2.cloned.1.call-done = f32[32,16,128]{2,1,0:T(8,128)} async-done(((f32[32,16,128]{2,1,0:T(8,128)}), f32[32,16,128]{2,1,0:T(8,128)}) %all-reduce.2.cloned.1.call-update) | async-done | bytes 262160 | tf_op jit(solution)/shard_map/psum | solution.py:41
  151.0 1.1 multiply_reduce_fusion
  152.1 1.8 broadcast_divide_fusion
  153.9 10.2 %all-to-all-start.1 = ((f32[32,16,128]{2,1,0:T(8,128)}), f32[32,16,128]{2,1,0:T(8,128)S(1)}, u32[]{:S(2)}, u32[]{:S(2)}) async-start(f32[32,16,128]{2,1,0:T(8,128)} %broadcast_divide_fusion), calls=%async_computation.1 | async-start | bytes 524288 | tf_op jit(solution)/shard_map/all_to_all | solution.py:59
  164.1 1.1 fusion.5
  165.3 0.8 fusion.41
  166.1 11.9 %all-to-all-done.1 = f32[32,16,128]{2,1,0:T(8,128)S(1)} async-done(((f32[32,16,128]{2,1,0:T(8,128)}), f32[32,16,128]{2,1,0:T(8,128)S(1)}, u32[]{:S(2)}, u32[]{:S(2)}) %all-to-all-start.1) | async-done | bytes 262176 | tf_op jit(solution)/shard_map/all_to_all | solution.py:59
  178.0 2.7 %scatter_custom_fusion.1 = f32[2048,128]{1,0:T(8,128)S(1)} fusion(s32[512]{0:T(512)S(1)} %bitcast.61, f32[512,128]{1,0:T(8,128)S(1)} %bitcast.59, f32[]{:T(128)} %constant.13.clone.1), kind=kCustom, calls=%fused_computation.15 | custom fusion | flops 65536 | bytes 1048580 | tf_op jit(solution)/shard_map/scatter-add | solution.py:67
  180.6 1.3 convolution_bitcast_fusion
  182.5 1.0 fusion.33
  183.8 0.8 copy-done.4
  184.7 1.3 fusion.4
  (37 shorter events, 4.4 us)
Async XLA Ops:
  7.2 2.2 %copy-start.2 = (bf16[1,64,4096]{2,1,0:T(8,128)(2,1)S(1)}, bf16[1,64,4096]{2,1,0:T(8,128)(2,1)}, u32[]{:S(2)}) copy-start(bf16[1,64,4096]{2,1,0:T(8,128)(2,1)} %param.6) | copy-start | bytes 1572868
  15.7 25.9 %all-to-all-start = ((f32[32,16,128]{2,1,0:T(8,128)}), f32[32,16,128]{2,1,0:T(8,128)S(1)}, u32[]{:S(2)}, u32[]{:S(2)}) async-start(f32[32,16,128]{2,1,0:T(8,128)} %broadcast_multiply_fusion), calls=%async_computation | async-start | bytes 524288 | tf_op jit(solution)/shard_map/all_to_all | solution.py:57
  28.9 0.7 copy-start.6
  28.9 122.1 %all-reduce.2.cloned.1.call-start = ((), (), s32[]{:S(2)}) async-start(), calls=%async_computation.2 | async-start | bytes 524288 | tf_op jit(solution)/shard_map/psum | solution.py:41
  41.5 0.7 copy-start.3
  43.5 120.7 %copy-start = (f32[1,64,4096]{2,1,0:T(8,128)S(1)}, f32[1,64,4096]{2,1,0:T(8,128)}, u32[]{:S(2)}) copy-start(f32[1,64,4096]{2,1,0:T(8,128)} %param.7) | copy-start | bytes 3145732
  153.9 24.0 %all-to-all-start.1 = ((f32[32,16,128]{2,1,0:T(8,128)}), f32[32,16,128]{2,1,0:T(8,128)S(1)}, u32[]{:S(2)}, u32[]{:S(2)}) async-start(f32[32,16,128]{2,1,0:T(8,128)} %broadcast_divide_fusion), calls=%async_computation.1 | async-start | bytes 524288 | tf_op jit(solution)/shard_map/all_to_all | solution.py:59
  164.1 1.1 copy-start.1
  183.5 1.0 copy-start.4
  183.6 1.2 copy-start.5
Sparse Core Ops, SparseCore 0:
  42.4 108.5 all-reduce.1
where the time goes:
time: 193 us
  waiting for transfers between devices  127 us (66%)
  starting transfers between devices  23.4 us (12%)
  between operations  14.3 us (7%)
  other arithmetic  12.8 us (7%)
  local copies, waits for them, and re-layouts  8.35 us (4%)
  matrix products  7.44 us (4%)
    psum x1, waiting for transfers between devices, island_norm(): total = lax.psum(pieces, 'island')  108 us
    all_to_all x1, starting transfers between devices, shards(): lax.all_to_all(chosen, 'fsdp', split_axis=0, concat_axis=0, tiled=True)  13.2 us
    all_to_all x1, waiting for transfers between devices, shards(): lax.all_to_all(compressed, 'fsdp', split_axis=0, concat_axis=0, tiled=True)  11.9 us
    all_to_all x1, starting transfers between devices, shards(): lax.all_to_all(compressed, 'fsdp', split_axis=0, concat_axis=0, tiled=True)  10.2 us
    all_to_all x1, waiting for transfers between devices, shards(): lax.all_to_all(chosen, 'fsdp', split_axis=0, concat_axis=0, tiled=True)  7.21 us
  transfers between devices with their start and end apart: 3, of which 3 were waited for; matrix products, arithmetic and copies ran while one was open for 4% of the time, Pallas kernels for 0%

commit v1 on v0

--- a/solution.py
+++ b/solution.py
@@ -38,7 +38,9 @@
 
 
 def island_norm(pieces):
-    total = lax.psum(pieces, "island")
+    total = pieces
+    for hop in (1, 2, 4, 8):
+        total = total + lax.ppermute(total, "island", [(dev, dev ^ hop) for dev in range(16)])
     return normalize(total)
 
 

time: 193 us -> 109 us (0.56)
  waiting for transfers between devices: 127 us -> 41.2 us
  blocking collectives: 0 us -> 25.6 us
  between operations: 14.3 us -> 0.92 us
  starting transfers between devices: 23.4 us -> 16.1 us
  other arithmetic: 12.8 us -> 10.1 us
    psum x1 -> x0, waiting for transfers between devices: 108 us -> none  [island_norm(): total = lax.psum(pieces, 'island')]
    ppermute x0 -> x4, waiting for transfers between devices: none -> 30.4 us  [island_norm(): lax.ppermute(total, 'island', [(dev, dev ^ hop) for dev in range(16)])]
    all_to_all x0 -> x1, blocking collectives: none -> 25.6 us  [shards(): lax.all_to_all(chosen, 'fsdp', split_axis=0, concat_axis=0, tiled=True)]
    all_to_all x1 -> x0, starting transfers between devices: 13.2 us -> none  [shards(): lax.all_to_all(chosen, 'fsdp', split_axis=0, concat_axis=0, tiled=True)]
    ppermute x0 -> x4, starting transfers between devices: none -> 11.8 us  [island_norm(): lax.ppermute(total, 'island', [(dev, dev ^ hop) for dev in range(16)])]
    all_to_all x1 -> x0, waiting for transfers between devices: 7.21 us -> none  [shards(): lax.all_to_all(chosen, 'fsdp', split_axis=0, concat_axis=0, tiled=True)]
    all_to_all x1, starting transfers between devices: 10.2 us -> 4.27 us  [shards(): lax.all_to_all(compressed, 'fsdp', split_axis=0, concat_axis=0, tiled=True)]
  transfers between devices with their start and end apart: 3 -> 5, of which waited for: 3 -> 5; matrix products, arithmetic and copies ran while one was open for 4% -> 7% of each run, Pallas kernels for 0% -> 0%
where the time goes in v1:
time: 109 us; the launch traced here: 108 us
  waiting for transfers between devices  41.2 us (38%)
  blocking collectives  25.6 us (23%)
  starting transfers between devices  16.1 us (15%)
  other arithmetic  10.1 us (9%)
  matrix products  7.44 us (7%)
  local copies, waits for them, and re-layouts  7.08 us (6%)
    ppermute x4, waiting for transfers between devices, island_norm(): lax.ppermute(total, 'island', [(dev, dev ^ hop) for dev in range(16)])  30.4 us
    all_to_all x1, blocking collectives, shards(): lax.all_to_all(chosen, 'fsdp', split_axis=0, concat_axis=0, tiled=True)  25.6 us
    ppermute x4, starting transfers between devices, island_norm(): lax.ppermute(total, 'island', [(dev, dev ^ hop) for dev in range(16)])  11.8 us
    all_to_all x1, waiting for transfers between devices, shards(): lax.all_to_all(compressed, 'fsdp', split_axis=0, concat_axis=0, tiled=True)  10.9 us
    all_to_all x1, starting transfers between devices, shards(): lax.all_to_all(compressed, 'fsdp', split_axis=0, concat_axis=0, tiled=True)  4.27 us
    dot_general x2, matrix products, inverse(): jnp.einsum('kn,rqkj->rnqj', table, blocks, precision=lax.Precision.HIGHEST)  2.6 us
    scatter-add x1, other arithmetic, shards(): jnp.zeros(coefficients.shape, jnp.float32).at[flat_ids]  2.5 us
    scatter x1, local copies, waits for them, and re-layouts, shards(): jnp.zeros((coefficients.shape[0],), jnp.float32).at[flat_ids]  2.45 us
  transfers between devices with their start and end apart: 5, of which 5 were waited for; matrix products, arithmetic and copies ran while one was open for 7% of the time, Pallas kernels for 0%

profile of v1, /device:TPU:24, one launch (start us, length us, event | category | flops | bytes accessed | tf_op | source)
XLA Modules:
  0.0 108.5 jit_solution(1053918347027110130)
XLA Ops:
  2.9 1.3 %fusion.6 = f32[8,8,32,128]{3,1,2,0:T(8,128)S(1)} fusion(bf16[1,64,4096]{2,1,0:T(8,128)(2,1)S(1)} %copy-done.1, f32[1,64,4096]{2,1,0:T(8,128)} %param.7), kind=kLoop, calls=%fused_computation.14 | loop fusion | flops 786432 | bytes 2621440
  4.4 1.7 %fusion.2 = f32[64,32,128]{2,0,1:T(8,128)S(1)} fusion(f32[128,128,1]{1,0,2:T(8,128)S(1)} %reshape.288, f32[64,32,128]{2,1,0:T(8,128)S(1)} %bitcast.56), kind=kOutput, calls=%fused_computation.7 | convolution fusion | flops 402653184 | bytes 2162688 | tf_op jit(solution)/shard_map/dot_general | solution.py:22
  6.0 1.2 %fusion.12 = f32[32,128,64]{1,2,0:T(8,128)S(1)} fusion(f32[64,32,128]{2,0,1:T(8,128)S(1)} %fusion.2, f32[64]{0:T(128)S(1)} %iota_convert_fusion, f32[64]{0:T(128)S(1)} %get-tuple-element.9, f32[64]{0:T(128)S(1)} %get-tuple-element.8), kind=kOutput, calls=%fused_computation.24 | convolution fusion | flops 201338880 | bytes 2097920 | tf_op jit(solution)/shard_map/kn,rnqj->rqkj/dot_general | solution.py:24
  7.3 1.0 gather_fusion
  8.4 25.6 %all_to_all.10 = f32[32,16,128]{2,1,0:T(8,128)S(1)} all-to-all(f32[32,16,128]{2,1,0:T(8,128)S(1)} %broadcast_multiply_fusion), channel_id=1, replica_groups=mesh['island'=16,'fsdp'=32] {'fsdp'}, dimensions={0} | all-to-all | bytes 524288 | tf_op jit(solution)/shard_map/all_to_all | solution.py:59
  34.1 2.0 %collective-permute-start = (f32[32,16,128]{2,1,0:T(8,128)S(1)}, f32[32,16,128]{2,1,0:T(8,128)S(1)}, u32[]{:S(2)}, u32[]{:S(2)}) collective-permute-start(f32[32,16,128]{2,1,0:T(8,128)S(1)} %all_to_all.10), channel_id=1, source_target_pairs={{0,32},{32,0},{64,96},{96,64},{128,160},{160,128},{192,224},{224,1... | collective-permute-start | bytes 786440 | tf_op jit(solution)/shard_map/ppermute | solution.py:43
  36.2 1.5 %collective-permute-done = f32[32,16,128]{2,1,0:T(8,128)S(1)} collective-permute-done((f32[32,16,128]{2,1,0:T(8,128)S(1)}, f32[32,16,128]{2,1,0:T(8,128)S(1)}, u32[]{:S(2)}, u32[]{:S(2)}) %collective-permute-start) | collective-permute-done | bytes 262176 | tf_op jit(solution)/shard_map/ppermute | solution.py:43
  37.7 2.4 %collective-permute-start.1 = (f32[32,16,128]{2,1,0:T(8,128)S(1)}, f32[32,16,128]{2,1,0:T(8,128)S(1)}, u32[]{:S(2)}, u32[]{:S(2)}) collective-permute-start(f32[32,16,128]{2,1,0:T(8,128)S(1)} %add.89), channel_id=1, source_target_pairs={{0,64},{32,96},{64,0},{96,32},{128,192},{160,224},{192,128},{224,1... | collective-permute-start | bytes 786440 | tf_op jit(solution)/shard_map/ppermute | solution.py:43
  40.2 7.7 %collective-permute-done.1 = f32[32,16,128]{2,1,0:T(8,128)S(1)} collective-permute-done((f32[32,16,128]{2,1,0:T(8,128)S(1)}, f32[32,16,128]{2,1,0:T(8,128)S(1)}, u32[]{:S(2)}, u32[]{:S(2)}) %collective-permute-start.1) | collective-permute-done | bytes 262176 | tf_op jit(solution)/shard_map/ppermute | solution.py:43
  48.0 2.2 %collective-permute-start.2 = (f32[32,16,128]{2,1,0:T(8,128)S(1)}, f32[32,16,128]{2,1,0:T(8,128)S(1)}, u32[]{:S(2)}, u32[]{:S(2)}) collective-permute-start(f32[32,16,128]{2,1,0:T(8,128)S(1)} %add.90), channel_id=1, source_target_pairs={{0,128},{32,160},{64,192},{96,224},{128,0},{160,32},{192,64},{224,... | collective-permute-start | bytes 786440 | tf_op jit(solution)/shard_map/ppermute | solution.py:43
  50.4 2.4 %scatter_custom_fusion = f32[2048]{0:T(1024)S(1)} fusion(s32[512]{0:T(512)S(1)} %bitcast.60, f32[512]{0:T(512)S(1)} %reshape.275, f32[]{:T(128)} %constant.13.clone.1), kind=kCustom, calls=%fused_computation.46 | custom fusion | bytes 8196 | tf_op jit(solution)/shard_map/scatter | solution.py:63
  53.0 1.3 %convolution_bitcast_fusion.1 = f32[1,64,32,128]{3,1,2,0:T(8,128)S(1)} fusion(f32[32,128,64]{1,2,0:T(8,128)S(1)} %fusion.12, f32[32,64]{1,0:T(8,128)S(1)} %mul.237, f32[64]{0:T(128)S(1)} %iota_convert_fusion, f32[64]{0:T(128)S(1)} %get-tuple-element.9, f32[64]{0:T(128)S(1)} %get-tuple-element.8), kind=kOutput, calls=%fused_computation.4 | convolution fusion | flops 201601024 | bytes 2106112 | tf_op jit(solution)/shard_map/kn,rqkj->rnqj/dot_general | solution.py:31
  54.9 8.9 %collective-permute-done.2 = f32[32,16,128]{2,1,0:T(8,128)S(1)} collective-permute-done((f32[32,16,128]{2,1,0:T(8,128)S(1)}, f32[32,16,128]{2,1,0:T(8,128)S(1)}, u32[]{:S(2)}, u32[]{:S(2)}) %collective-permute-start.2) | collective-permute-done | bytes 262176 | tf_op jit(solution)/shard_map/ppermute | solution.py:43
  63.8 5.2 %collective-permute-start.3 = (f32[32,16,128]{2,1,0:T(8,128)S(1)}, f32[32,16,128]{2,1,0:T(8,128)S(1)}, u32[]{:S(2)}, u32[]{:S(2)}) collective-permute-start(f32[32,16,128]{2,1,0:T(8,128)S(1)} %add.91), channel_id=1, source_target_pairs={{0,256},{32,288},{64,320},{96,352},{128,384},{160,416},{192,448},{... | collective-permute-start | bytes 786440 | tf_op jit(solution)/shard_map/ppermute | solution.py:43
  69.0 1.0 fusion.32
  70.2 12.3 %collective-permute-done.3 = f32[32,16,128]{2,1,0:T(8,128)S(1)} collective-permute-done((f32[32,16,128]{2,1,0:T(8,128)S(1)}, f32[32,16,128]{2,1,0:T(8,128)S(1)}, u32[]{:S(2)}, u32[]{:S(2)}) %collective-permute-start.3) | collective-permute-done | bytes 262176 | tf_op jit(solution)/shard_map/ppermute | solution.py:43
  82.6 0.8 broadcast_divide_fusion
  83.5 4.3 %all-to-all-start.1 = ((f32[32,16,128]{2,1,0:T(8,128)}), f32[32,16,128]{2,1,0:T(8,128)S(1)}, u32[]{:S(2)}, u32[]{:S(2)}) async-start(f32[32,16,128]{2,1,0:T(8,128)} %broadcast_divide_fusion), calls=%async_computation.1 | async-start | bytes 524288 | tf_op jit(solution)/shard_map/all_to_all | solution.py:61
  87.8 1.1 %fusion.5 = f32[1,64,4096]{2,1,0:T(8,128)} fusion(f32[1,64,4096]{2,1,0:T(8,128)S(1)} %reshape.256, bf16[1,64,4096]{2,1,0:T(8,128)(2,1)S(1)} %copy-done.1, f32[1,64,4096]{2,1,0:T(8,128)S(1)} %copy-done), kind=kLoop, calls=%fused_computation.13 | loop fusion | flops 1048576 | bytes 3670016 | tf_op jit(solution)/shard_map/sub | solution.py:65
  89.7 10.9 %all-to-all-done.1 = f32[32,16,128]{2,1,0:T(8,128)S(1)} async-done(((f32[32,16,128]{2,1,0:T(8,128)}), f32[32,16,128]{2,1,0:T(8,128)S(1)}, u32[]{:S(2)}, u32[]{:S(2)}) %all-to-all-start.1) | async-done | bytes 262176 | tf_op jit(solution)/shard_map/all_to_all | solution.py:61
  100.6 2.5 %scatter_custom_fusion.1 = f32[2048,128]{1,0:T(8,128)S(1)} fusion(s32[512]{0:T(512)S(1)} %bitcast.61, f32[512,128]{1,0:T(8,128)S(1)} %bitcast.59, f32[]{:T(128)} %constant.13.clone.1), kind=kCustom, calls=%fused_computation.15 | custom fusion | flops 65536 | bytes 1048580 | tf_op jit(solution)/shard_map/scatter-add | solution.py:69
  103.1 1.3 %convolution_bitcast_fusion = f32[1,64,32,128]{3,1,2,0:T(8,128)S(1)} fusion(f32[32,64,128]{2,1,0:T(8,128)S(1)} %bitcast.55, f32[64]{0:T(128)S(1)} %iota_convert_fusion, f32[64]{0:T(128)S(1)} %get-tuple-element.9, f32[64]{0:T(128)S(1)} %get-tuple-element.8), kind=kOutput, calls=%fused_computation.3 | convolution fusion | flops 201338880 | bytes 2097920 | tf_op jit(solution)/shard_map/kn,rqkj->rnqj/dot_general | solution.py:31
  105.0 1.0 fusion.33
  107.2 1.3 %fusion.4 = (bf16[64,4096]{1,0:T(8,128)(2,1)}, bf16[64,4096]{1,0:T(8,128)(2,1)}) fusion(f32[64,4096]{1,0:T(8,128)S(1)} %reshape.261, bf16[64,4096]{1,0:T(8,128)(2,1)S(1)} %copy-done.2, bf16[64,4096]{1,0:T(8,128)(2,1)S(1)} %copy-done.3), kind=kLoop, calls=%fused_computation.11 | loop fusion | flops 2621440 | bytes 3145728 | tf_op jit(solution)/shard_map/convert_element_type | solution.py:73
  (40 shorter events, 6.6 us)
Async XLA Ops:
  0.6 2.2 %copy-start.1 = (bf16[1,64,4096]{2,1,0:T(8,128)(2,1)S(1)}, bf16[1,64,4096]{2,1,0:T(8,128)(2,1)}, u32[]{:S(2)}) copy-start(bf16[1,64,4096]{2,1,0:T(8,128)(2,1)} %param.6) | copy-start | bytes 1572868
  34.1 6.0 %copy-start.4 = (s32[1,32,16]{1,2,0:T(8,128)S(1)}, s32[1,32,16]{1,2,0:T(8,128)}, u32[]{:S(2)}) copy-start(s32[1,32,16]{1,2,0:T(8,128)} %param.10) | copy-start | bytes 6148
  34.1 3.5 %collective-permute-start = (f32[32,16,128]{2,1,0:T(8,128)S(1)}, f32[32,16,128]{2,1,0:T(8,128)S(1)}, u32[]{:S(2)}, u32[]{:S(2)}) collective-permute-start(f32[32,16,128]{2,1,0:T(8,128)S(1)} %all_to_all.10), channel_id=1, source_target_pairs={{0,32},{32,0},{64,96},{96,64},{128,160},{160,128},{192,224},{224,1... | collective-permute-start | bytes 786440 | tf_op jit(solution)/shard_map/ppermute | solution.py:43
  37.7 10.2 %collective-permute-start.1 = (f32[32,16,128]{2,1,0:T(8,128)S(1)}, f32[32,16,128]{2,1,0:T(8,128)S(1)}, u32[]{:S(2)}, u32[]{:S(2)}) collective-permute-start(f32[32,16,128]{2,1,0:T(8,128)S(1)} %add.89), channel_id=1, source_target_pairs={{0,64},{32,96},{64,0},{96,32},{128,192},{160,224},{192,128},{224,1... | collective-permute-start | bytes 786440 | tf_op jit(solution)/shard_map/ppermute | solution.py:43
  48.0 15.8 %collective-permute-start.2 = (f32[32,16,128]{2,1,0:T(8,128)S(1)}, f32[32,16,128]{2,1,0:T(8,128)S(1)}, u32[]{:S(2)}, u32[]{:S(2)}) collective-permute-start(f32[32,16,128]{2,1,0:T(8,128)S(1)} %add.90), channel_id=1, source_target_pairs={{0,128},{32,160},{64,192},{96,224},{128,0},{160,32},{192,64},{224,... | collective-permute-start | bytes 786440 | tf_op jit(solution)/shard_map/ppermute | solution.py:43
  63.8 18.7 %collective-permute-start.3 = (f32[32,16,128]{2,1,0:T(8,128)S(1)}, f32[32,16,128]{2,1,0:T(8,128)S(1)}, u32[]{:S(2)}, u32[]{:S(2)}) collective-permute-start(f32[32,16,128]{2,1,0:T(8,128)S(1)} %add.91), channel_id=1, source_target_pairs={{0,256},{32,288},{64,320},{96,352},{128,384},{160,416},{192,448},{... | collective-permute-start | bytes 786440 | tf_op jit(solution)/shard_map/ppermute | solution.py:43
  70.2 17.6 %copy-start = (f32[1,64,4096]{2,1,0:T(8,128)S(1)}, f32[1,64,4096]{2,1,0:T(8,128)}, u32[]{:S(2)}) copy-start(f32[1,64,4096]{2,1,0:T(8,128)} %param.7) | copy-start | bytes 3145732
  83.5 17.1 %all-to-all-start.1 = ((f32[32,16,128]{2,1,0:T(8,128)}), f32[32,16,128]{2,1,0:T(8,128)S(1)}, u32[]{:S(2)}, u32[]{:S(2)}) async-start(f32[32,16,128]{2,1,0:T(8,128)} %broadcast_divide_fusion), calls=%async_computation.1 | async-start | bytes 524288 | tf_op jit(solution)/shard_map/all_to_all | solution.py:61
  106.0 1.0 copy-start.2
  106.0 1.2 %copy-start.3 = (bf16[64,4096]{1,0:T(8,128)(2,1)S(1)}, bf16[64,4096]{1,0:T(8,128)(2,1)}, u32[]{:S(2)}) copy-start(bf16[64,4096]{1,0:T(8,128)(2,1)} %param.8) | copy-start | bytes 1572868
